TPU v7x, 256 devices: a whole 4x4x8 slice. The times are simulated.
256 devices in a mesh: gz: 8 (over z_lo, core), gy: 32 (over z_hi, x, y).
Axes of the slice: x: 4, y: 4, z: 8 (z_hi: 2, z_lo: 4; z = z_hi * 4 + z_lo), core: 2. Of those that a mesh axis runs over, the one named last changes fastest.
Arguments:
- features: bfloat16 [64, 16, 64, 128], P(None, 'gz', 'gy'), may hold values from -6 to 6
- up_weight: bfloat16 [64, 32, 4, 4, 4], replicated, may hold values from -0.25 to 0.25
- conv_weight: bfloat16 [32, 32, 3, 3, 3], replicated, may hold values from -0.21875 to 0.21875
- out_grad: bfloat16 [32, 32, 128, 256], P(None, 'gz', 'gy'), may hold values from -6 to 6
- labels: int32 [32, 128, 256], P('gz', 'gy'), may hold values 0 or 1
Outputs:
- decoded: bfloat16 [32, 32, 128, 256], P(None, 'gz', 'gy')
- features_grad: bfloat16 [64, 16, 64, 128], P(None, 'gz', 'gy')
- up_weight_grad: float32 [64, 32, 4, 4, 4], replicated
- conv_weight_grad: float32 [32, 32, 3, 3, 3], replicated
Inputs may be any that keep to these rules, and one draw needn't show every extreme that they name: `labels`: 1 marks an annotated voxel, 0 an unannotated one.
All inputs are finite; a program needn't handle non-finite values. No bound on the sum of `labels` on one device may be relied on, other than what follows from the above.
Results may differ from a plain program's by a relative error of at most 0.02.
Values may be sent and summed in bfloat16 or wider, within the bound.
A program may use at most 64 MiB of HBM per device.

v0:
```python
import math

import jax
import jax.numpy as jnp
from jax import lax
from jax.sharding import PartitionSpec as P

forward_specs = ("NCDHW", "OIDHW", "NCDHW")
kernel_specs = ("CNDHW", "IODHW", "NCDHW")


def from_behind(block, axis, distance):
    devices = range(lax.axis_size(axis))
    route = [(i - distance, i) for i in devices if i - distance in devices]
    return lax.ppermute(block, axis, route)


def with_halo(block, sides, width):
    for axis, dim in sides:
        count = lax.axis_size(axis)
        forward = [(i, i + 1) for i in range(count - 1)]
        backward = [(target, source) for source, target in forward]
        low = lax.ppermute(
            lax.slice_in_dim(block, block.shape[dim] - width, None, axis=dim), axis, forward
        )
        high = lax.ppermute(lax.slice_in_dim(block, 0, width, axis=dim), axis, backward)
        block = jnp.concatenate([low, block, high], axis=dim)
    return block


def convolve(lhs, rhs, strides, padding, lhs_dilation, rhs_dilation, specs):
    return lax.conv_general_dilated(
        lhs[None],
        rhs,
        window_strides=strides,
        padding=padding,
        lhs_dilation=lhs_dilation,
        rhs_dilation=rhs_dilation,
        dimension_numbers=specs,
        preferred_element_type=jnp.float32,
    )


def lift_kernel(up_weight):
    return jnp.flip(jnp.transpose(up_weight, (1, 0, 2, 3, 4)), (2, 3, 4))


def stencil(rimmed, weight):
    return convolve(
        rimmed, weight, (1, 1, 1), ((0, 0), (0, 0), (1, 1)), (1, 1, 1), (1, 1, 1), forward_specs
    )[0]


def shards(features, up_weight, conv_weight, out_grad, labels):
    extent_z = out_grad.shape[1]
    extent_y = out_grad.shape[2]
    extent_x = out_grad.shape[3]
    coarse_z = features.shape[1]
    coarse_y = features.shape[2]
    coarse_x = features.shape[3]
    kernel = lift_kernel(up_weight)
    spread = convolve(
        features, kernel, (1, 1, 1), ((3, 3), (3, 3), (2, 2)), (2, 2, 2), (1, 1, 1), forward_specs
    )[0]
    from_below = from_behind(spread[:, -1:], "gz", 1)
    from_above = from_behind(spread[:, :1], "gz", -1)
    middle = spread[:, 1:-1]
    middle = jnp.concatenate(
        [middle[:, :1] + from_below, middle[:, 1:-1], middle[:, -1:] + from_above], axis=1
    )
    from_left = from_behind(middle[:, :, -1:], "gy", 1)
    from_right = from_behind(middle[:, :, :1], "gy", -1)
    interior = middle[:, :, 1:-1]
    lifted = jnp.concatenate(
        [interior[:, :, :1] + from_left, interior[:, :, 1:-1], interior[:, :, -1:] + from_right],
        axis=2,
    )
    hidden = jnp.maximum(lifted, 0.0).astype(jnp.bfloat16)
    hidden_rimmed = with_halo(hidden, (("gz", 1), ("gy", 2)), 1)
    decoded = stencil(hidden_rimmed, conv_weight).astype(jnp.bfloat16)
    cotangent = out_grad * labels.astype(jnp.bfloat16)[None]
    back_weight = jnp.transpose(jnp.flip(conv_weight, (2, 3, 4)), (1, 0, 2, 3, 4))
    cotangent_rimmed = with_halo(cotangent, (("gz", 1), ("gy", 2)), 1)
    before = stencil(cotangent_rimmed, back_weight)
    hidden_grad = jnp.where(hidden > 0, before, 0.0).astype(jnp.bfloat16)
    grad_rimmed = with_halo(hidden_grad, (("gz", 1), ("gy", 2)), 1)
    conv_terms = convolve(
        hidden_rimmed,
        cotangent[None],
        (1, 1, 1),
        ((0, 0), (0, 0), (1, 1)),
        (1, 1, 1),
        (1, 1, 1),
        kernel_specs,
    )
    conv_terms = jnp.transpose(conv_terms, (1, 0, 2, 3, 4))
    features_grad = convolve(
        grad_rimmed,
        up_weight,
        (2, 2, 2),
        ((0, 0), (0, 0), (1, 1)),
        (1, 1, 1),
        (1, 1, 1),
        forward_specs,
    )[0]
    up_terms = convolve(
        grad_rimmed,
        features[None],
        (1, 1, 1),
        ((0, 0), (0, 0), (1, 1)),
        (1, 1, 1),
        (2, 2, 2),
        kernel_specs,
    )
    up_terms = jnp.transpose(up_terms, (1, 0, 2, 3, 4))
    up_sum, conv_sum = lax.psum((up_terms, conv_terms), ("gz", "gy"))
    devices = lax.axis_size("gz") * lax.axis_size("gy")
    up_grad = up_sum * (1.0 / math.sqrt(coarse_z * coarse_y * coarse_x * devices))
    conv_grad = conv_sum * (1.0 / math.sqrt(extent_z * extent_y * extent_x * devices))
    return (decoded, features_grad.astype(jnp.bfloat16), up_grad, conv_grad)


def solution(mesh):
    in_specs = (P(None, "gz", "gy", None), P(), P(), P(None, "gz", "gy", None), P("gz", "gy", None))
    out_specs = (P(None, "gz", "gy", None), P(None, "gz", "gy", None), P(), P())
    return jax.shard_map(shards, mesh=mesh, in_specs=in_specs, out_specs=out_specs, check_vma=False)
```

profile of v0, /device:TPU:1, one launch (start us, length us, event | category | flops | bytes accessed | tf_op | source)
XLA Modules:
  0.0 505.5 jit_solution(6629715965674340061)
XLA Ops:
  9.0 4.9 collective-permute-start.8
  17.1 13.5 %broadcast_select_fusion = f32[6,6,8,34,32]{4,2,3,1,0:T(8,128)} fusion(pred[8,34]{0,1:T(8,128)(4,1)} %constant.29, bf16[64,32,4,4,4]{0,4,3,2,1:T(4,128)(2,1)S(1)} %copy-done, bf16[64,2,2,1,7,2]{0,4,5,2,1,3:T(8,128)(2,1)S(1)} %slice.104, bf16[64,2,2,1,8,17]{0,4,5,2,1,3:T(8,128)(2,1)S(1)} %copy.70), kind=kOutput, calls=%fused_computation.20 | convolution fusion | flops 143153152 | bytes 1592592 | tf_op jit(solution)/shard_map/conv_general_dilated | solution.py:32
  30.6 6.2 %copy.72 = f32[6,6,8,34,32]{3,2,4,1,0:T(8,128)} copy(f32[6,6,8,34,32]{4,2,3,1,0:T(8,128)} %broadcast_select_fusion) | data formatting | bytes 2506752 | tf_op jit(solution)/shard_map/conv_general_dilated | solution.py:32
  36.7 3.9 reshape.17
  40.8 3.6 collective-permute-start
  50.8 3.8 copy.89
  59.1 3.6 reshape.59
  62.7 3.7 copy.79
  71.0 5.2 %fusion.9 = bf16[4,4,8,33,32]{4,2,3,1,0:T(8,128)(2,1)S(1)} fusion(bf16[32,32,3,3,3]{1,0,4,3,2:T(8,128)(2,1)} %param.7, bf16[32,6,6,1,7,2]{0,4,5,2,1,3:T(8,128)(2,1)S(1)} %slice.120, bf16[32,6,6,1,8,33]{0,4,5,2,1,3:T(8,128)(2,1)} %copy.79), kind=kOutput, calls=%fused_computation.10 | convolution fusion | flops 235505664 | bytes 966144 | tf_op jit(solution)/shard_map/conv_general_dilated | solution.py:32
  84.9 4.1 collective-permute-done.3
  94.1 3.6 collective-permute-start.4
  99.8 4.4 collective-permute-start.14
  105.6 4.0 collective-permute-start.6
  111.2 8.2 %copy.86 = bf16[1,32,6,6,256]{1,0,4,3,2:T(2,128)(2,1)} copy(bf16[1,32,6,6,256]{4,1,3,2,0:T(8,128)(2,1)S(1)} %get-tuple-element.32) | data formatting | bytes 1179648 | tf_op jit(solution)/shard_map/broadcast_in_dim | solution.py:33
  119.5 8.1 %copy.88 = bf16[1,32,6,6,256]{1,0,4,3,2:T(2,128)(2,1)} copy(bf16[1,32,6,6,256]{4,1,3,2,0:T(8,128)(2,1)S(1)} %get-tuple-element.30) | data formatting | bytes 1179648 | tf_op jit(solution)/shard_map/broadcast_in_dim | solution.py:33
  128.9 3.5 reshape.34
  132.4 3.7 copy.83
  137.1 3.3 fusion.27
  142.5 3.5 reshape.20
  146.0 3.7 copy.74
  150.6 4.9 fusion.13
  158.3 14.3 %fusion.64 = f32[64,32,4,4,4]{0,1,4,3,2:T(8,128)} fusion(bf16[1,32,6,6,256]{1,0,4,3,2:T(2,128)(2,1)} %copy.86, bf16[1,64,2,2,128]{1,0,4,3,2:T(2,128)(2,1)S(1)} %copy-done.9), kind=kOutput, calls=%fused_computation.86 | convolution fusion | flops 133693440 | bytes 1179648 | tf_op jit(solution)/shard_map/transpose | solution.py:115
  172.6 31.3 %fusion.65 = f32[32,32,3,3,3]{0,1,4,3,2:T(8,128)} fusion(bf16[1,32,6,6,256]{1,0,4,3,2:T(2,128)(2,1)} %copy.88, bf16[1,32,4,4,256]{1,0,4,3,2:T(2,128)(2,1)S(1)} %copy-done.4), kind=kOutput, calls=%fused_computation.87 | convolution fusion | flops 225902592 | bytes 962560 | tf_op jit(solution)/shard_map/transpose | solution.py:96
  207.2 287.1 %all-reduce.3.cloned.1.call-done = (f32[64,32,4,4,4]{0,1,4,3,2:T(8,128)}, f32[32,32,3,3,3]{0,1,4,3,2:T(8,128)}) async-done(((f32[64,32,4,4,4]{0,1,4,3,2:T(8,128)}, f32[32,32,3,3,3]{0,1,4,3,2:T(8,128)}), (f32[64,32,4,4,4]{0,1,4,3,2:T(8,128)}, f32[32,32,3,3,3]{0,1,4,3,2:T(8,128)})) %all-reduce.3.cloned.1.call-update) | async-done | bytes 634896 | tf_op jit(solution)/shard_map/psum | solution.py:116
  (105 shorter events, 54.6 us)
Async XLA Ops:
  7.2 9.9 %copy-start = (bf16[64,32,4,4,4]{0,4,3,2,1:T(4,128)(2,1)S(1)}, bf16[64,32,4,4,4]{0,4,3,2,1:T(4,128)(2,1)}, u32[]{:S(2)}) copy-start(bf16[64,32,4,4,4]{0,4,3,2,1:T(4,128)(2,1)} %param.6) | copy-start | bytes 786436
  7.2 487.1 %all-reduce.3.cloned.1.call-start = ((), (), s32[]{:S(2)}) async-start(), calls=%async_computation | async-start | bytes 2981888 | tf_op jit(solution)/shard_map/psum | solution.py:116
  9.0 35.4 %collective-permute-start.8 = (bf16[32,1,4,256]{3,2,1,0:T(4,128)(2,1)S(1)}, bf16[32,1,4,256]{3,2,1,0:T(4,128)(2,1)S(1)}, u32[]{:S(2)}, u32[]{:S(2)}) collective-permute-start(bf16[32,1,4,256]{3,2,1,0:T(4,128)(2,1)S(1)} %get-tuple-element.44), channel_id=1, source_target_pairs={{0,32},{32,64},{64,96},{96,128},{128,160},{160,192},{192,224},{1,3... | collective-permute-start | bytes 196616 | tf_op jit(solution)/shard_map/ppermute | solution.py:23
  14.0 30.5 %collective-permute-start.9 = (bf16[32,1,4,256]{3,2,1,0:T(4,128)(2,1)S(1)}, bf16[32,1,4,256]{3,2,1,0:T(4,128)(2,1)S(1)}, u32[]{:S(2)}, u32[]{:S(2)}) collective-permute-start(bf16[32,1,4,256]{3,2,1,0:T(4,128)(2,1)S(1)} %get-tuple-element.45), channel_id=1, source_target_pairs={{32,0},{64,32},{96,64},{128,96},{160,128},{192,160},{224,192},{33,... | collective-permute-start | bytes 196616 | tf_op jit(solution)/shard_map/ppermute | solution.py:26
  40.6 9.1 %copy-start.5 = (bf16[32,4,4,256]{3,2,1,0:T(4,128)(2,1)S(1)}, bf16[32,4,4,256]{3,2,1,0:T(4,128)(2,1)}, u32[]{:S(2)}) copy-start(bf16[32,4,4,256]{3,2,1,0:T(4,128)(2,1)} %param.8) | copy-start | bytes 786436
  40.6 9.3 %copy-start.8 = (bf16[64,2,2,128]{3,2,1,0:T(2,128)(2,1)S(1)}, bf16[64,2,2,128]{3,2,1,0:T(2,128)(2,1)}, u32[]{:S(2)}) copy-start(bf16[64,2,2,128]{3,2,1,0:T(2,128)(2,1)} %param.5) | copy-start | bytes 196612
  40.7 9.1 %copy-start.2 = (f32[32,6,6,256]{3,0,2,1:T(8,128)}, f32[32,6,6,256]{3,0,2,1:T(8,128)S(1)}, u32[]{:S(2)}) copy-start(f32[32,6,6,256]{3,0,2,1:T(8,128)S(1)} %slice_bitcast_fusion) | copy-start | bytes 3538948
  40.8 26.6 %collective-permute-start = (f32[32,1,6,256]{3,0,2,1:T(8,128)S(1)}, f32[32,1,6,256]{3,0,2,1:T(8,128)}, u32[]{:S(2)}, u32[]{:S(2)}) collective-permute-start(f32[32,1,6,256]{3,0,2,1:T(8,128)S(1)} %slice.107), channel_id=1, source_target_pairs={{0,32},{32,64},{64,96},{96,128},{128,160},{160,192},{192,224},{1,3... | collective-permute-start | bytes 589832 | tf_op jit(solution)/shard_map/ppermute | solution.py:15
  45.0 9.6 %collective-permute-start.10 = (bf16[32,6,1,256]{3,2,1,0:T(2,128)(2,1)S(1)}, bf16[32,6,1,256]{3,2,1,0:T(2,128)(2,1)S(1)}, u32[]{:S(2)}, u32[]{:S(2)}) collective-permute-start(bf16[32,6,1,256]{3,2,1,0:T(2,128)(2,1)S(1)} %get-tuple-element.38), channel_id=1, source_target_pairs={{0,1},{1,2},{2,3},{3,4},{4,5},{5,6},{6,7},{7,8},{8,9},{9,10},{10,1... | collective-permute-start | bytes 294920 | tf_op jit(solution)/shard_map/ppermute | solution.py:23
  48.2 8.6 %collective-permute-start.11 = (bf16[32,6,1,256]{3,2,1,0:T(2,128)(2,1)S(1)}, bf16[32,6,1,256]{3,2,1,0:T(2,128)(2,1)S(1)}, u32[]{:S(2)}, u32[]{:S(2)}) collective-permute-start(bf16[32,6,1,256]{3,2,1,0:T(2,128)(2,1)S(1)} %get-tuple-element.39), channel_id=1, source_target_pairs={{1,0},{2,1},{3,2},{4,3},{5,4},{6,5},{7,6},{8,7},{9,8},{10,9},{11,1... | collective-permute-start | bytes 294920 | tf_op jit(solution)/shard_map/ppermute | solution.py:26
  68.5 8.8 %collective-permute-start.1 = (f32[32,1,6,256]{3,0,2,1:T(8,128)S(1)}, f32[32,1,6,256]{3,0,2,1:T(8,128)}, u32[]{:S(2)}, u32[]{:S(2)}) collective-permute-start(f32[32,1,6,256]{3,0,2,1:T(8,128)S(1)} %get-tuple-element.25), channel_id=1, source_target_pairs={{32,0},{64,32},{96,64},{128,96},{160,128},{192,160},{224,192},{33,... | collective-permute-start | bytes 589832 | tf_op jit(solution)/shard_map/ppermute | solution.py:15
  76.2 6.7 %copy-start.10 = (pred[8,33]{1,0:T(8,128)(4,1)S(1)}, pred[8,33]{1,0:T(8,128)(4,1)}, u32[]{:S(2)}) copy-start(pred[8,33]{1,0:T(8,128)(4,1)} %constant.28) | copy-start | bytes 796
  78.4 6.4 %collective-permute-start.2 = (f32[32,4,1,256]{3,0,2,1:T(8,128)S(1)}, f32[32,4,1,256]{3,0,2,1:T(8,128)S(1)}, u32[]{:S(2)}, u32[]{:S(2)}) collective-permute-start(f32[32,4,1,256]{3,0,2,1:T(8,128)S(1)} %get-tuple-element.28), channel_id=1, source_target_pairs={{0,1},{1,2},{2,3},{3,4},{4,5},{5,6},{6,7},{7,8},{8,9},{9,10},{10,1... | collective-permute-start | bytes 393224 | tf_op jit(solution)/shard_map/ppermute | solution.py:15
  81.6 7.3 %collective-permute-start.3 = (f32[32,4,1,256]{3,0,2,1:T(8,128)S(1)}, f32[32,4,1,256]{3,0,2,1:T(8,128)S(1)}, u32[]{:S(2)}, u32[]{:S(2)}) collective-permute-start(f32[32,4,1,256]{3,0,2,1:T(8,128)S(1)} %get-tuple-element.29), channel_id=1, source_target_pairs={{1,0},{2,1},{3,2},{4,3},{5,4},{6,5},{7,6},{8,7},{9,8},{10,9},{11,1... | collective-permute-start | bytes 393224 | tf_op jit(solution)/shard_map/ppermute | solution.py:15
  89.1 10.6 %collective-permute-start.12 = (bf16[32,1,4,256]{3,0,2,1:T(8,128)(2,1)S(1)}, bf16[32,1,4,256]{3,0,2,1:T(8,128)(2,1)S(1)}, u32[]{:S(2)}, u32[]{:S(2)}) collective-permute-start(bf16[32,1,4,256]{3,0,2,1:T(8,128)(2,1)S(1)} %get-tuple-element.40), channel_id=1, source_target_pairs={{0,32},{32,64},{64,96},{96,128},{128,160},{160,192},{192,224},{1,3... | collective-permute-start | bytes 196616 | tf_op jit(solution)/shard_map/ppermute | solution.py:23
  92.2 7.5 %collective-permute-start.13 = (bf16[32,1,4,256]{3,0,2,1:T(8,128)(2,1)S(1)}, bf16[32,1,4,256]{3,0,2,1:T(8,128)(2,1)S(1)}, u32[]{:S(2)}, u32[]{:S(2)}) collective-permute-start(bf16[32,1,4,256]{3,0,2,1:T(8,128)(2,1)S(1)} %get-tuple-element.41), channel_id=1, source_target_pairs={{32,0},{64,32},{96,64},{128,96},{160,128},{192,160},{224,192},{33,... | collective-permute-start | bytes 196616 | tf_op jit(solution)/shard_map/ppermute | solution.py:26
  94.1 11.4 %collective-permute-start.4 = (bf16[32,1,4,256]{3,0,2,1:T(8,128)(2,1)S(1)}, bf16[32,1,4,256]{3,0,2,1:T(8,128)(2,1)S(1)}, u32[]{:S(2)}, u32[]{:S(2)}) collective-permute-start(bf16[32,1,4,256]{3,0,2,1:T(8,128)(2,1)S(1)} %get-tuple-element.42), channel_id=1, source_target_pairs={{0,32},{32,64},{64,96},{96,128},{128,160},{160,192},{192,224},{1,3... | collective-permute-start | bytes 196616 | tf_op jit(solution)/shard_map/ppermute | solution.py:23
  97.8 7.7 %collective-permute-start.5 = (bf16[32,1,4,256]{3,0,2,1:T(8,128)(2,1)S(1)}, bf16[32,1,4,256]{3,0,2,1:T(8,128)(2,1)S(1)}, u32[]{:S(2)}, u32[]{:S(2)}) collective-permute-start(bf16[32,1,4,256]{3,0,2,1:T(8,128)(2,1)S(1)} %get-tuple-element.43), channel_id=1, source_target_pairs={{32,0},{64,32},{96,64},{128,96},{160,128},{192,160},{224,192},{33,... | collective-permute-start | bytes 196616 | tf_op jit(solution)/shard_map/ppermute | solution.py:26
  99.8 11.3 %collective-permute-start.14 = (bf16[32,6,1,256]{3,0,2,1:T(8,128)(2,1)S(1)}, bf16[32,6,1,256]{3,0,2,1:T(8,128)(2,1)S(1)}, u32[]{:S(2)}, u32[]{:S(2)}) collective-permute-start(bf16[32,6,1,256]{3,0,2,1:T(8,128)(2,1)S(1)} %get-tuple-element.34), channel_id=1, source_target_pairs={{0,1},{1,2},{2,3},{3,4},{4,5},{5,6},{6,7},{7,8},{8,9},{9,10},{10,1... | collective-permute-start | bytes 294920 | tf_op jit(solution)/shard_map/ppermute | solution.py:23
  104.2 6.9 %collective-permute-start.15 = (bf16[32,6,1,256]{3,0,2,1:T(8,128)(2,1)S(1)}, bf16[32,6,1,256]{3,0,2,1:T(8,128)(2,1)S(1)}, u32[]{:S(2)}, u32[]{:S(2)}) collective-permute-start(bf16[32,6,1,256]{3,0,2,1:T(8,128)(2,1)S(1)} %get-tuple-element.35), channel_id=1, source_target_pairs={{1,0},{2,1},{3,2},{4,3},{5,4},{6,5},{7,6},{8,7},{9,8},{10,9},{11,1... | collective-permute-start | bytes 294920 | tf_op jit(solution)/shard_map/ppermute | solution.py:26
  105.6 13.8 %collective-permute-start.6 = (bf16[32,6,1,256]{3,0,2,1:T(8,128)(2,1)S(1)}, bf16[32,6,1,256]{3,0,2,1:T(8,128)(2,1)S(1)}, u32[]{:S(2)}, u32[]{:S(2)}) collective-permute-start(bf16[32,6,1,256]{3,0,2,1:T(8,128)(2,1)S(1)} %get-tuple-element.36), channel_id=1, source_target_pairs={{0,1},{1,2},{2,3},{3,4},{4,5},{5,6},{6,7},{7,8},{8,9},{9,10},{10,1... | collective-permute-start | bytes 294920 | tf_op jit(solution)/shard_map/ppermute | solution.py:23
  109.6 9.8 %collective-permute-start.7 = (bf16[32,6,1,256]{3,0,2,1:T(8,128)(2,1)S(1)}, bf16[32,6,1,256]{3,0,2,1:T(8,128)(2,1)S(1)}, u32[]{:S(2)}, u32[]{:S(2)}) collective-permute-start(bf16[32,6,1,256]{3,0,2,1:T(8,128)(2,1)S(1)} %get-tuple-element.37), channel_id=1, source_target_pairs={{1,0},{2,1},{3,2},{4,3},{5,4},{6,5},{7,6},{8,7},{9,8},{10,9},{11,1... | collective-permute-start | bytes 294920 | tf_op jit(solution)/shard_map/ppermute | solution.py:26
  158.3 14.3 %copy-start.4 = (bf16[1,32,4,4,256]{1,0,4,3,2:T(2,128)(2,1)S(1)}, bf16[1,32,4,4,256]{1,0,4,3,2:T(2,128)(2,1)}, u32[]{:S(2)}) copy-start(bf16[1,32,4,4,256]{1,0,4,3,2:T(2,128)(2,1)} %copy.89) | copy-start | bytes 786436
  172.6 31.4 %copy-start.6 = (bf16[2,2,8,17,64]{4,1,3,2,0:T(2,128)(2,1)S(1)}, bf16[2,2,8,17,64]{4,1,3,2,0:T(2,128)(2,1)}, u32[]{:S(2)}) copy-start(bf16[2,2,8,17,64]{4,1,3,2,0:T(2,128)(2,1)} %copy.85) | copy-start | bytes 208900
  (6 other events, 20.6 us)
Sparse Core Ops, SparseCore 0:
  204.0 290.2 all-reduce.2
where the time goes:
time: 515 us; the launch traced here: 505 us
  waiting for transfers between devices  294 us (57%)
  matrix products  72.4 us (14%)
  local copies, waits for them, and re-layouts  71.9 us (14%)
  starting transfers between devices  43.9 us (9%)
  between operations  14.9 us (3%)
  other arithmetic  8.53 us (2%)
    psum x1, waiting for transfers between devices, shards(): up_sum, conv_sum = lax.psum((up_terms, conv_terms), ('gz', 'gy'))  287 us
    conv_general_dilated x17, local copies, waits for them, and re-layouts, convolve(): lax.conv_general_dilated(lhs[None], rhs, window_strides=strides, padding=...  38.4 us
    transpose x1, matrix products, shards(): conv_terms = jnp.transpose(conv_terms, (1, 0, 2, 3, 4))  31.3 us
    conv_general_dilated x4, matrix products, convolve(): lax.conv_general_dilated(lhs[None], rhs, window_strides=strides, padding=...  26.8 us
    ppermute x6, starting transfers between devices, with_halo(): lax.ppermute(lax.slice_in_dim(block, block.shape[dim] - width, None, axis...  23.3 us
    broadcast_in_dim x7, local copies, waits for them, and re-layouts, convolve(): lhs[None]  21.4 us
    transpose x1, matrix products, shards(): up_terms = jnp.transpose(up_terms, (1, 0, 2, 3, 4))  14.3 us
    ppermute x4, starting transfers between devices, from_behind(): return lax.ppermute(block, axis, route)  10.6 us
  transfers between devices with their start and end apart: 17, of which 4 were waited for; matrix products, arithmetic and copies ran while one was open for 12% of the time, Pallas kernels for 0%

commit v1 on v0

v1 whole, which is shorter than its diff:
```python
import math

import jax
import jax.numpy as jnp
from jax import lax
from jax.experimental import pallas as pl
from jax.experimental.pallas import tpu as pltpu
from jax.sharding import PartitionSpec as P

BF = jnp.bfloat16
F32 = jnp.float32
MESH = pl.DeviceIdType.MESH

NZ, NY = 8, 32
DIRECTIONS = [(dz, dy) for dz in (-1, 0, 1) for dy in (-1, 0, 1) if (dz, dy) != (0, 0)]
PIECE = 48
HALF = 16 * PIECE


def mm(a, b):
    return lax.dot_general(a, b, (((1,), (0,)), ((), ())), preferred_element_type=F32)


def mm_nt(a, b):
    return lax.dot_general(a, b, (((1,), (1,)), ((), ())), preferred_element_type=F32)


def mm_tn(a, b):
    return lax.dot_general(a, b, (((0,), (0,)), ((), ())), preferred_element_type=F32)


def one_hot(rows, cols, place):
    row = lax.broadcasted_iota(jnp.int32, (rows, cols), 0)
    col = lax.broadcasted_iota(jnp.int32, (rows, cols), 1)
    return jnp.where(place(row) == col, 1.0, 0.0).astype(BF)


def lane_masks(rows):
    lane = lax.broadcasted_iota(jnp.int32, (rows, 128), 1)
    return lane == 0, lane == 127


def before_lane(x, first):
    return jnp.where(first, 0.0, pltpu.roll(x, 1, 1))


def after_lane(x, last):
    return jnp.where(last, 0.0, pltpu.roll(x, 127, 1))


def halo_source(step, extent):
    if step == 0:
        return pl.ds(1, extent)
    return pl.ds(extent, 1) if step == 1 else pl.ds(1, 1)


def halo_target(step, extent):
    if step == 0:
        return pl.ds(1, extent)
    return pl.ds(0, 1) if step == 1 else pl.ds(extent + 1, 1)


def kernel(
    feat_ref, up_ref, conv_ref, og_ref, lab_ref,
    dec_ref, fgrad_ref, ugrad_ref, cgrad_ref,
    fh, ch, gh, fx, hx, cx, hgx, he,
    upf, uwt, t_up, t_fwd, t_bwd, dec,
    part, got0, pair, got1, got2, full,
    f_send, f_recv, c_send, c_recv, g_send, g_recv,
    s0_send, s0_recv, s1_send, s1_recv, s2_send, s2_recv, s3_send, s3_recv, s4_send, s4_recv,
):
    gz = lax.axis_index("gz")
    gy = lax.axis_index("gy")
    core = gz % 2
    z_lo = gz // 2
    z_hi = gy // 16
    xy = gy % 16
    chip_z = z_hi * 4 + z_lo
    partner = (gz + 1 - 2 * core, gy)

    def xy_peer(step):
        q = (xy + step) % 16
        return q, (gz, z_hi * 16 + q)

    def z_peer(step):
        q = (chip_z + step) % 8
        return q, ((q % 4) * 2 + core, (q // 4) * 16 + xy)

    def exists(dz, dy):
        return (gz + dz >= 0) & (gz + dz < NZ) & (gy + dy >= 0) & (gy + dy < NY)

    for buf, n in ((fh, 2), (ch, 4), (gh, 4)):
        for line in (0, n + 1):
            buf[line] = jnp.zeros(buf.shape[1:], BF)
            for k in range(1, n + 1):
                buf[k, line] = jnp.zeros(buf.shape[2:], BF)

    barrier = pltpu.get_barrier_semaphore()
    for dz, dy in DIRECTIONS:
        @pl.when(exists(dz, dy))
        def _():
            pl.semaphore_signal(barrier, 1, device_id=(gz + dz, gy + dy), device_id_type=MESH)
    pl.semaphore_signal(barrier, 1, device_id=partner, device_id_type=MESH)

    @pl.loop(1, 16)
    def _(step):
        pl.semaphore_signal(barrier, 1, device_id=xy_peer(step)[1], device_id_type=MESH)

    @pl.loop(1, 8)
    def _(step):
        pl.semaphore_signal(barrier, 1, device_id=z_peer(step)[1], device_id_type=MESH)

    local = mm(one_hot(256, 256, lambda r: (r & 63) * 4 + (r >> 6)), feat_ref[...]).astype(BF)
    for k in range(4):
        fh[1 + k // 2, 1 + k % 2] = local[k * 64 : (k + 1) * 64]
    split = one_hot(256, 256, lambda r: (r & 1) * 128 + (r >> 1))
    masked = (og_ref[...].reshape(32, 16, 256) * lab_ref[...].astype(BF)[None]).reshape(512, 256)
    rows = mm(one_hot(512, 512, lambda r: (r & 31) * 16 + (r >> 5)), masked).astype(BF)
    local = mm(rows, split).astype(BF)
    for k in range(16):
        ch[1 + k // 4, 1 + k % 4] = local[k * 32 : (k + 1) * 32]

    beside = 1 * (gz > 0) + 1 + 1 * (gz < NZ - 1)
    beside = beside * (1 * (gy > 0) + 1 + 1 * (gy < NY - 1)) - 1
    pl.semaphore_wait(barrier, beside + 1 + 15 + 7)

    def halo_copy(buf, extent, index, send, recv):
        dz, dy = DIRECTIONS[index]
        return pltpu.make_async_remote_copy(
            src_ref=buf.at[halo_source(dz, extent), halo_source(dy, extent)],
            dst_ref=buf.at[halo_target(dz, extent), halo_target(dy, extent)],
            send_sem=send.at[index],
            recv_sem=recv.at[index],
            device_id=(gz + dz, gy + dy),
            device_id_type=MESH,
        )

    def halo_start(*what):
        for index, (dz, dy) in enumerate(DIRECTIONS):
            @pl.when(exists(dz, dy))
            def _():
                halo_copy(what[0], what[1], index, what[2], what[3]).start()

    def halo_arrived(*what):
        for index, (dz, dy) in enumerate(DIRECTIONS):
            @pl.when(exists(-dz, -dy))
            def _():
                halo_copy(what[0], what[1], index, what[2], what[3]).wait_recv()

    def halo_sent(*what):
        for index, (dz, dy) in enumerate(DIRECTIONS):
            @pl.when(exists(dz, dy))
            def _():
                halo_copy(what[0], what[1], index, what[2], what[3]).wait_send()

    f_halo = (fh, 2, f_send, f_recv)
    c_halo = (ch, 4, c_send, c_recv)
    g_halo = (gh, 4, g_send, g_recv)
    halo_start(*f_halo)
    halo_start(*c_halo)

    upf[...] = up_ref[...].astype(F32)

    @pl.loop(0, 64)
    def _(k):
        uwt[k] = upf[pl.ds(k, 32, stride=64), :].astype(BF)

    for sz in range(2):
        for sy in range(2):
            for px in range(2):
                blocks = []
                for uz in range(2):
                    for uy in range(2):
                        base = (2 * (1 - uz) + sz) * 16 + (2 * (1 - uy) + sy) * 4
                        none = jnp.zeros((32, 64), BF)
                        if px == 0:
                            blocks += [uwt[base + 3], uwt[base + 1], none]
                        else:
                            blocks += [none, uwt[base + 2], uwt[base]]
                at = ((sz * 2 + sy) * 2 + px) * 32
                t_up[at : at + 32, :] = jnp.concatenate(blocks, axis=1)
    zero = jnp.zeros((32, 96), BF)
    taps = {}
    back = {}
    for dz in range(3):
        for dy in range(3):
            at = (dz * 3 + dy) * 96
            taps[dz, dy] = jnp.concatenate(
                [conv_ref[at + 32 * dx : at + 32 * dx + 32, :] for dx in range(3)], axis=1
            )
            back[2 - dz, 2 - dy] = conv_ref[at : at + 96, :].T
    for yo in range(4):
        for matrix, source in ((t_fwd, taps), (t_bwd, back)):
            matrix[yo * 32 : yo * 32 + 32, :] = jnp.concatenate(
                [
                    source[dz, yi - yo] if 0 <= yi - yo < 3 else zero
                    for dz in range(3)
                    for yi in range(6)
                ],
                axis=1,
            )

    halo_arrived(*f_halo)
    first64, last64 = lane_masks(64)
    first, last = lane_masks(32)
    for k in range(16):
        row = fh[k // 4, k % 4]
        wide = row.astype(F32)
        fx[k, 0:64] = before_lane(wide, first64).astype(BF)
        fx[k, 64:128] = row
        fx[k, 128:192] = after_lane(wide, last64).astype(BF)

    @pl.loop(0, 3)
    def _(jz):
        columns = []
        for jy in range(3):
            columns.append(
                jnp.concatenate(
                    [fx[(jz + uz) * 4 + jy + uy] for uz in range(2) for uy in range(2)], axis=0
                )
            )
        lifted = jnp.maximum(mm(t_up[...], jnp.concatenate(columns, axis=1)), 0.0)
        for sz in range(2):
            for sy in range(2):
                for jy in range(3):
                    at = (sz * 2 + sy) * 64
                    even = lifted[at : at + 32, jy * 128 : jy * 128 + 128]
                    odd = lifted[at + 32 : at + 64, jy * 128 : jy * 128 + 128]
                    zo, yo = jz * 2 + sz, jy * 2 + sy
                    at = pl.multiple_of((zo * 6 + yo) * 96, 32)
                    even_b, odd_b = even.astype(BF), odd.astype(BF)
                    hx[pl.ds(at, 32), 0:128] = before_lane(odd, first).astype(BF)
                    hx[pl.ds(at, 32), 128:256] = even_b
                    hx[pl.ds(at + 32, 32), 0:128] = even_b
                    hx[pl.ds(at + 32, 32), 128:256] = odd_b
                    hx[pl.ds(at + 64, 32), 0:128] = odd_b
                    hx[pl.ds(at + 64, 32), 128:256] = after_lane(even, last).astype(BF)
                    he[zo, yo, :, 0:128] = even_b
                    he[zo, yo, :, 128:256] = odd_b

    @pl.when(gz == 0)
    def _():
        hx[0:576] = jnp.zeros((576, 256), BF)

    @pl.when(gz == NZ - 1)
    def _():
        hx[2880:3456] = jnp.zeros((576, 256), BF)

    @pl.when(gy == 0)
    def _():
        for zi in range(6):
            hx[zi * 576 : zi * 576 + 96] = jnp.zeros((96, 256), BF)

    @pl.when(gy == NY - 1)
    def _():
        for zi in range(6):
            hx[zi * 576 + 480 : zi * 576 + 576] = jnp.zeros((96, 256), BF)

    halo_arrived(*c_halo)

    @pl.loop(0, 6)
    def _(zi):
        for yi in range(6):
            row = ch[zi, yi]
            even_b, odd_b = row[:, 0:128], row[:, 128:256]
            at = pl.multiple_of((zi * 6 + yi) * 96, 32)
            cx[pl.ds(at, 32), 0:128] = odd_b
            cx[pl.ds(at, 32), 128:256] = after_lane(even_b.astype(F32), last).astype(BF)
            cx[pl.ds(at + 32, 32), :] = row
            cx[pl.ds(at + 64, 32), 0:128] = before_lane(odd_b.astype(F32), first).astype(BF)
            cx[pl.ds(at + 64, 32), 128:256] = even_b

    @pl.loop(0, 4)
    def _(zo):
        before = mm(t_bwd[...], cx[pl.ds(pl.multiple_of(zo * 576, 32), 1728), :])
        for yo in range(4):
            grad = jnp.where(
                he[1 + zo, 1 + yo].astype(F32) > 0.0, before[yo * 32 : yo * 32 + 32], 0.0
            )
            gh[1 + zo, 1 + yo] = grad.astype(BF)

    halo_start(*g_halo)

    def spread_grad(row, slot):
        even, odd = row[:, 0:128], row[:, 128:256]
        hgx[slot, 0:32] = before_lane(odd.astype(F32), first).astype(BF)
        hgx[slot, 32:64] = even
        hgx[slot, 64:96] = odd
        hgx[slot, 96:128] = after_lane(even.astype(F32), last).astype(BF)

    for zi in range(1, 5):
        for yi in range(1, 5):
            spread_grad(gh[zi, yi], zi * 6 + yi)

    for sz in range(2):
        for sy in range(2):
            lhs, rhs = [], []
            for jz in (0, 1) if sz else (1, 2):
                for jy in (0, 1) if sy else (1, 2):
                    lhs.append(hgx[(2 * jz + sz) * 6 + 2 * jy + sy])
                    rhs.append(
                        jnp.concatenate(
                            [fh[jz + 1 - vz, jy + 1 - vy] for vz in range(2) for vy in range(2)],
                            axis=0,
                        )
                    )
            grad = mm_nt(jnp.concatenate(lhs, axis=1), jnp.concatenate(rhs, axis=1)).astype(BF)
            at = (sz * 2 + sy) * 256
            part[at : at + 128] = grad[:, 0:128]
            part[at + 128 : at + 256] = grad[:, 128:256]
    part[1024:1536] = jnp.zeros((512, 128), BF)
    for dz in range(3):
        total = jnp.zeros((128, 576), F32)
        for zo in range(4):
            total = total + mm_nt(
                ch[1 + zo, 1:5].reshape(128, 256), hx[(zo + dz) * 576 : (zo + dz + 1) * 576, :]
            )
        for dy in range(3):
            grad = total[0:32, dy * 96 : dy * 96 + 96]
            for yo in range(1, 4):
                grad = grad + total[yo * 32 : yo * 32 + 32, (yo + dy) * 96 : (yo + dy) * 96 + 96]
            at = 1024 + (dz * 3 + dy) * 32
            part[at : at + 32, 0:96] = grad.astype(BF)

    def remote(src, dst, send, recv, device):
        return pltpu.make_async_remote_copy(
            src_ref=src, dst_ref=dst, send_sem=send, recv_sem=recv,
            device_id=device, device_id_type=MESH,
        )

    mine = pl.multiple_of(core * HALF, 16)
    other = pl.multiple_of((1 - core) * HALF, 16)
    copy0 = remote(part.at[pl.ds(other, HALF)], got0, s0_send, s0_recv, partner)
    copy0.start()

    @pl.loop(0, 4)
    def _(zo):
        done = mm(t_fwd[...], hx[pl.ds(pl.multiple_of(zo * 576, 32), 1728), :])
        dec[pl.ds(pl.multiple_of(zo * 128, 16), 128), :] = done.astype(BF)

    copy0.wait()
    pair[...] = (part[pl.ds(mine, HALF), :].astype(F32) + got0[...].astype(F32)).astype(BF)

    def copy1(step):
        q, device = xy_peer(step)
        return remote(
            pair.at[pl.ds(pl.multiple_of(q * PIECE, 16), PIECE)], got1.at[xy],
            s1_send.at[step], s1_recv.at[step], device,
        )

    @pl.loop(1, 16)
    def _(step):
        copy1(step).start()

    got1[xy] = pair[pl.ds(pl.multiple_of(xy * PIECE, 16), PIECE), :]
    joined = mm_nt(dec[...], split).astype(BF)
    order = one_hot(512, 512, lambda r: (r & 15) * 32 + (r >> 4))
    dec_ref[...] = mm(order, joined).astype(BF)

    @pl.loop(1, 16)
    def _(step):
        copy1(step).wait()

    total = got1[0].astype(F32)
    for k in range(1, 16):
        total = total + got1[k].astype(F32)
    got2[chip_z] = total.astype(BF)

    def copy2(step):
        _, device = z_peer(step)
        return remote(
            got2.at[chip_z], got2.at[chip_z], s2_send.at[step], s2_recv.at[step], device
        )

    @pl.loop(1, 8)
    def _(step):
        copy2(step).start()

    halo_arrived(*g_halo)
    for zi in range(6):
        for yi in range(6):
            if zi in (0, 5) or yi in (0, 5):
                spread_grad(gh[zi, yi], zi * 6 + yi)
    back_up = uwt[...].reshape(2048, 64)
    flat = []
    for iz in range(2):
        columns = []
        for iy in range(2):
            columns.append(
                jnp.concatenate(
                    [
                        hgx[(2 * iz + kz) * 6 + 2 * iy + ky]
                        for kz in range(4)
                        for ky in range(4)
                    ],
                    axis=0,
                )
            )
        both = mm_tn(back_up, jnp.concatenate(columns, axis=1)).astype(BF)
        flat += [both[:, 0:128], both[:, 128:256]]
    order = one_hot(256, 256, lambda r: (r & 3) * 64 + (r >> 2))
    fgrad_ref[...] = mm(order, jnp.concatenate(flat, axis=0)).astype(BF)

    @pl.loop(1, 8)
    def _(step):
        copy2(step).wait()

    total = got2[0].astype(F32)
    for k in range(1, 8):
        total = total + got2[k].astype(F32)
    spot = pl.multiple_of(mine + xy * PIECE, 16)
    full[pl.ds(spot, PIECE), :] = total.astype(BF)

    def copy3(step):
        _, device = xy_peer(step)
        here = full.at[pl.ds(spot, PIECE)]
        return remote(here, here, s3_send.at[step], s3_recv.at[step], device)

    @pl.loop(1, 16)
    def _(step):
        copy3(step).start()

    @pl.loop(1, 16)
    def _(step):
        copy3(step).wait()

    here = full.at[pl.ds(mine, HALF)]
    copy4 = remote(here, here, s4_send, s4_recv, partner)
    copy4.start()
    halo_sent(*f_halo)
    halo_sent(*c_halo)
    halo_sent(*g_halo)
    copy4.wait()

    scale = 1.0 / math.sqrt(131072)
    for sz in range(2):
        for vz in range(2):
            for sy in range(2):
                at = ((sz * 2 + sy) * 2 + vz) * 128
                for kx in range(4):
                    rows = full[at + kx * 32 : at + kx * 32 + 32, :].astype(F32) * scale
                    for vy in range(2):
                        k = (2 * vz + sz) * 16 + (2 * vy + sy) * 4 + kx
                        ugrad_ref[pl.ds(k, 32, stride=64), :] = rows[:, vy * 64 : vy * 64 + 64]
    scale = 1.0 / math.sqrt(1048576)
    for k in range(9):
        rows = full[1024 + k * 32 : 1024 + k * 32 + 32, :].astype(F32) * scale
        for dx in range(3):
            at = (k * 3 + dx) * 32
            cgrad_ref[at : at + 32, :] = rows[:, dx * 32 : dx * 32 + 32]


def shards(features, up_weight, conv_weight, out_grad, labels):
    dma = pltpu.SemaphoreType.DMA
    vmem = pltpu.VMEM
    decoded, features_grad, up_grad, conv_grad = pl.pallas_call(
        kernel,
        out_shape=(
            jax.ShapeDtypeStruct((512, 256), BF),
            jax.ShapeDtypeStruct((256, 128), BF),
            jax.ShapeDtypeStruct((2048, 64), F32),
            jax.ShapeDtypeStruct((864, 32), F32),
        ),
        in_specs=[pl.BlockSpec(memory_space=vmem)] * 5,
        out_specs=[pl.BlockSpec(memory_space=vmem)] * 4,
        scratch_shapes=[
            vmem((4, 4, 64, 128), BF),
            vmem((6, 6, 32, 256), BF),
            vmem((6, 6, 32, 256), BF),
            vmem((16, 192, 128), BF),
            vmem((3456, 256), BF),
            vmem((3456, 256), BF),
            vmem((36, 128, 128), BF),
            vmem((6, 6, 32, 256), BF),
            vmem((2048, 64), F32),
            vmem((64, 32, 64), BF),
            vmem((256, 768), BF),
            vmem((128, 1728), BF),
            vmem((128, 1728), BF),
            vmem((512, 256), BF),
            vmem((2 * HALF, 128), BF),
            vmem((HALF, 128), BF),
            vmem((HALF, 128), BF),
            vmem((16, PIECE, 128), BF),
            vmem((8, PIECE, 128), BF),
            vmem((2 * HALF, 128), BF),
            dma((8,)), dma((8,)), dma((8,)), dma((8,)), dma((8,)), dma((8,)),
            dma, dma, dma((16,)), dma((16,)), dma((8,)), dma((8,)), dma((16,)), dma((16,)), dma, dma,
        ],
        compiler_params=pltpu.CompilerParams(
            collective_id=0, has_side_effects=True, vmem_limit_bytes=48 * 1024 * 1024
        ),
        name="decoder_step",
    )(
        features.reshape(256, 128),
        jnp.transpose(up_weight, (1, 2, 3, 4, 0)).reshape(2048, 64),
        jnp.transpose(conv_weight, (2, 3, 4, 0, 1)).reshape(864, 32),
        out_grad.reshape(512, 256),
        labels.reshape(16, 256),
    )
    return (
        decoded.reshape(32, 4, 4, 256),
        features_grad.reshape(64, 2, 2, 128),
        jnp.transpose(up_grad.reshape(32, 4, 4, 4, 64), (4, 0, 1, 2, 3)),
        jnp.transpose(conv_grad.reshape(3, 3, 3, 32, 32), (3, 4, 0, 1, 2)),
    )


def solution(mesh):
    in_specs = (P(None, "gz", "gy", None), P(), P(), P(None, "gz", "gy", None), P("gz", "gy", None))
    out_specs = (P(None, "gz", "gy", None), P(None, "gz", "gy", None), P(), P())
    return jax.shard_map(shards, mesh=mesh, in_specs=in_specs, out_specs=out_specs, check_vma=False)
```

time: 515 us -> 56.5 us (0.11); the launches traced: 505 us -> 56.3 us
  waiting for transfers between devices: 294 us -> 0 us
  matrix products: 72.4 us -> 0 us
  local copies, waits for them, and re-layouts: 71.9 us -> 6.7 us
  Pallas kernels: 0 us -> 48.9 us
  starting transfers between devices: 43.9 us -> 0 us
  between operations: 14.9 us -> 0.67 us
  other arithmetic: 8.53 us -> 0 us
    psum x1 -> x0, waiting for transfers between devices: 287 us -> none  [shards(): up_sum, conv_sum = lax.psum((up_terms, conv_terms), ('gz', 'gy'))]
    pallas_call x0 -> x1, Pallas kernels: none -> 48.9 us  [shards(): pl.pallas_call(kernel, out_shape=(jax.ShapeDtypeStruct((512, 256), BF), j...]
    transpose x2 -> x0, matrix products: 45.6 us -> none  [the longest x1 31.3 us: shards(): conv_terms = jnp.transpose(conv_terms, (1, 0, 2, 3, 4))]
    ppermute x16 -> x0, starting transfers between devices: 43.9 us -> none  [the longest x6 23.3 us: with_halo(): lax.ppermute(lax.slice_in_dim(block, block.shape[dim] - width, None, axis...]
    conv_general_dilated x17 -> x0, local copies, waits for them, and re-layouts: 38.4 us -> none  [convolve(): lax.conv_general_dilated(lhs[None], rhs, window_strides=strides, padding=...]
    conv_general_dilated x4 -> x0, matrix products: 26.8 us -> none  [convolve(): lax.conv_general_dilated(lhs[None], rhs, window_strides=strides, padding=...]
    broadcast_in_dim x8 -> x0, local copies, waits for them, and re-layouts: 25.3 us -> none  [the longest x7 21.4 us: convolve(): lhs[None]]
    ppermute x16 -> x0, waiting for transfers between devices: 6.72 us -> none  [the longest x4 4.44 us: from_behind(): return lax.ppermute(block, axis, route)]
  transfers between devices with their start and end apart: 17 -> 0, of which waited for: 4 -> 0; matrix products, arithmetic and copies ran while one was open for 12% -> 0% of each run, Pallas kernels for 0% -> 0%
where the time goes in v1:
time: 56.5 us; the launch traced here: 56.3 us
  Pallas kernels  48.9 us (87%)
  local copies, waits for them, and re-layouts  6.7 us (12%)
  between operations  0.67 us (1%)
    pallas_call x1, Pallas kernels, shards(): pl.pallas_call(kernel, out_shape=(jax.ShapeDtypeStruct((512, 256), BF), j...  48.9 us
    unnamed x9, local copies, waits for them, and re-layouts  4.13 us

profile of v1, /device:TPU:1, one launch (start us, length us, event | category | flops | bytes accessed | tf_op | source)
XLA Modules:
  0.0 56.3 jit_solution(8469160832659822816)
XLA Ops:
  0.6 0.0 copy-start
  0.6 0.8 %reshape.39.lab_ref = s32[16,256]{1,0:T(8,128)S(1)} reshape(s32[4,4,256]{2,1,0:T(4,128)} %param.9) | data formatting | bytes 32768 | tf_op jit(solution)/shard_map/reshape | solution.py:499
  1.4 1.0 %reshape.38.og_ref = bf16[512,256]{1,0:T(8,128)(2,1)S(1)} reshape(bf16[32,4,4,256]{3,2,1,0:T(4,128)(2,1)} %param.8) | data formatting | bytes 524288 | tf_op jit(solution)/shard_map/reshape | solution.py:498
  2.4 0.0 copy-done
  2.5 0.0 copy-start.1
  2.5 0.9 %copy-done.1 = bf16[32,32,3,3,3]{1,0,4,3,2:T(8,128)(2,1)S(1)} copy-done((bf16[32,32,3,3,3]{1,0,4,3,2:T(8,128)(2,1)S(1)}, bf16[32,32,3,3,3]{1,0,4,3,2:T(8,128)(2,1)}, u32[]{:S(2)}) %copy-start.1) | copy-done | bytes 55320
  3.4 0.0 copy-start.2
  3.4 0.8 %copy-done.2 = bf16[64,2,2,128]{3,2,1,0:T(2,128)(2,1)S(1)} copy-done((bf16[64,2,2,128]{3,2,1,0:T(2,128)(2,1)S(1)}, bf16[64,2,2,128]{3,2,1,0:T(2,128)(2,1)}, u32[]{:S(2)}) %copy-start.2) | copy-done | bytes 65560
  4.2 48.9 %decoder_step.1 = (bf16[512,256]{1,0:T(8,128)(2,1)S(1)}, bf16[256,128]{1,0:T(8,128)(2,1)S(1)}, f32[2048,64]{1,0:T(8,128)S(1)}, f32[864,32]{1,0:T(8,128)S(1)}) custom-call(bf16[256,128]{1,0:T(8,128)(2,1)S(1)} %bitcast.18, bf16[2048,64]{1,0:T(8,128)(2,1)S(1)} %bitcast.15, bf16[864,32]{1,0:T(8,128)(2,1)S(1)} %bitcast.17, bf16[512,256]{1,0:T(8,128)(2,1)S(1)} %reshape.38.og_ref, ...), custom_call_target="tpu_custom_call" | custom-call | tf_op jit(solution)/shard_map/decoder_step/pallas_call | solution.py:456
  53.1 0.8 %reshape.40 = bf16[32,4,4,256]{3,2,1,0:T(4,128)(2,1)} reshape(bf16[512,256]{1,0:T(8,128)(2,1)S(1)} %get-tuple-element.8) | data formatting | bytes 524288 | tf_op jit(solution)/shard_map/reshape | solution.py:502
  53.9 0.6 %copy.12 = bf16[64,2,2,128]{3,2,1,0:T(2,128)(2,1)} copy(bf16[64,2,2,128]{3,2,1,0:T(2,128)(2,1)S(1)} %bitcast.19) | data formatting | bytes 131072
  54.5 1.0 %copy.13 = f32[64,32,4,4,4]{0,4,3,2,1:T(4,128)} copy(f32[64,32,4,4,4]{0,4,3,2,1:T(4,128)S(1)} %bitcast.14) | data formatting | bytes 1048576
  55.5 0.8 %copy.14 = f32[32,32,3,3,3]{1,0,4,3,2:T(8,128)} copy(f32[32,32,3,3,3]{1,0,4,3,2:T(8,128)S(1)} %bitcast.16) | data formatting | bytes 221184
Async XLA Ops:
  0.6 1.8 %copy-start = (bf16[64,32,4,4,4]{0,4,3,2,1:T(4,128)(2,1)S(1)}, bf16[64,32,4,4,4]{0,4,3,2,1:T(4,128)(2,1)}, u32[]{:S(2)}) copy-start(bf16[64,32,4,4,4]{0,4,3,2,1:T(4,128)(2,1)} %param.6) | copy-start | bytes 786436
  2.5 0.9 %copy-start.1 = (bf16[32,32,3,3,3]{1,0,4,3,2:T(8,128)(2,1)S(1)}, bf16[32,32,3,3,3]{1,0,4,3,2:T(8,128)(2,1)}, u32[]{:S(2)}) copy-start(bf16[32,32,3,3,3]{1,0,4,3,2:T(8,128)(2,1)} %param.7) | copy-start | bytes 165892
  3.4 0.8 %copy-start.2 = (bf16[64,2,2,128]{3,2,1,0:T(2,128)(2,1)S(1)}, bf16[64,2,2,128]{3,2,1,0:T(2,128)(2,1)}, u32[]{:S(2)}) copy-start(bf16[64,2,2,128]{3,2,1,0:T(2,128)(2,1)} %param.5) | copy-start | bytes 196612

commit v2 on v1

--- a/solution.py
+++ b/solution.py
@@ -13,6 +13,11 @@
 
 NZ, NY = 8, 32
 DIRECTIONS = [(dz, dy) for dz in (-1, 0, 1) for dy in (-1, 0, 1) if (dz, dy) != (0, 0)]
+XY_STEPS = sorted(
+    [(dx, dy) for dx in range(4) for dy in range(4) if (dx, dy) != (0, 0)],
+    key=lambda step: -(min(step[0], 4 - step[0]) + min(step[1], 4 - step[1])),
+)
+Z_STEPS = (4, 3, 5, 2, 6, 1, 7)
 PIECE = 48
 HALF = 16 * PIECE
 
@@ -61,8 +66,9 @@
 
 
 def kernel(
-    feat_ref, up_ref, conv_ref, og_ref, lab_ref,
+    feat_hbm, up_hbm, conv_hbm, og_hbm, lab_hbm,
     dec_ref, fgrad_ref, ugrad_ref, cgrad_ref,
+    feat_ref, up_ref, conv_ref, og_ref, lab_ref, load_sem,
     fh, ch, gh, fx, hx, cx, hgx, he,
     upf, uwt, t_up, t_fwd, t_bwd, dec,
     part, got0, pair, got1, got2, full,
@@ -79,44 +85,64 @@
     partner = (gz + 1 - 2 * core, gy)
 
     def xy_peer(step):
-        q = (xy + step) % 16
+        q = (xy // 4 + step[0]) % 4 * 4 + (xy % 4 + step[1]) % 4
         return q, (gz, z_hi * 16 + q)
 
     def z_peer(step):
         q = (chip_z + step) % 8
-        return q, ((q % 4) * 2 + core, (q // 4) * 16 + xy)
+        return (q % 4) * 2 + core, (q // 4) * 16 + xy
 
     def exists(dz, dy):
         return (gz + dz >= 0) & (gz + dz < NZ) & (gy + dy >= 0) & (gy + dy < NY)
-
-    for buf, n in ((fh, 2), (ch, 4), (gh, 4)):
-        for line in (0, n + 1):
-            buf[line] = jnp.zeros(buf.shape[1:], BF)
-            for k in range(1, n + 1):
-                buf[k, line] = jnp.zeros(buf.shape[2:], BF)
 
     barrier = pltpu.get_barrier_semaphore()
     for dz, dy in DIRECTIONS:
         @pl.when(exists(dz, dy))
         def _():
             pl.semaphore_signal(barrier, 1, device_id=(gz + dz, gy + dy), device_id_type=MESH)
+
+    loads = [
+        pltpu.make_async_copy(source, target, load_sem.at[index])
+        for index, (source, target) in enumerate(
+            (
+                (feat_hbm, feat_ref),
+                (og_hbm, og_ref),
+                (lab_hbm, lab_ref),
+                (up_hbm, up_ref),
+                (conv_hbm, conv_ref),
+            )
+        )
+    ]
+    for load in loads:
+        load.start()
     pl.semaphore_signal(barrier, 1, device_id=partner, device_id_type=MESH)
 
-    @pl.loop(1, 16)
-    def _(step):
+    for step in XY_STEPS:
         pl.semaphore_signal(barrier, 1, device_id=xy_peer(step)[1], device_id_type=MESH)
-
-    @pl.loop(1, 8)
-    def _(step):
-        pl.semaphore_signal(barrier, 1, device_id=z_peer(step)[1], device_id_type=MESH)
-
+    for step in Z_STEPS:
+        pl.semaphore_signal(barrier, 1, device_id=z_peer(step), device_id_type=MESH)
+
+    loads[0].wait()
     local = mm(one_hot(256, 256, lambda r: (r & 63) * 4 + (r >> 6)), feat_ref[...]).astype(BF)
     for k in range(4):
         fh[1 + k // 2, 1 + k % 2] = local[k * 64 : (k + 1) * 64]
+
     split = one_hot(256, 256, lambda r: (r & 1) * 128 + (r >> 1))
-    masked = (og_ref[...].reshape(32, 16, 256) * lab_ref[...].astype(BF)[None]).reshape(512, 256)
-    rows = mm(one_hot(512, 512, lambda r: (r & 31) * 16 + (r >> 5)), masked).astype(BF)
-    local = mm(rows, split).astype(BF)
+    loads[1].wait()
+    loads[2].wait()
+    masked = (og_ref[...].reshape(32, 32, 128) * lab_ref[...].astype(BF)[None]).reshape(1024, 128)
+    rows = mm(
+        one_hot(512, 512, lambda r: (r & 15) * 32 + (r >> 4)),
+        jnp.concatenate([masked[0:512], masked[512:1024]], axis=1),
+    ).astype(BF)
+    for k in range(16):
+        for half in range(2):
+            at = ((k // 4) * 8 + half * 4 + k % 4) * 16
+            for group in range(2):
+                dec[k * 32 + group * 16 : k * 32 + group * 16 + 16, half * 128 : half * 128 + 128] = (
+                    rows[at : at + 16, group * 128 : group * 128 + 128]
+                )
+    local = mm(dec[...], split).astype(BF)
     for k in range(16):
         ch[1 + k // 4, 1 + k % 4] = local[k * 32 : (k + 1) * 32]
 
@@ -159,6 +185,30 @@
     halo_start(*f_halo)
     halo_start(*c_halo)
 
+    @pl.when(gz == 0)
+    def _():
+        for buf in (fh, ch, gh):
+            buf[0] = jnp.zeros(buf.shape[1:], BF)
+
+    @pl.when(gz == NZ - 1)
+    def _():
+        for buf in (fh, ch, gh):
+            buf[buf.shape[0] - 1] = jnp.zeros(buf.shape[1:], BF)
+
+    @pl.when(gy == 0)
+    def _():
+        for buf in (fh, ch, gh):
+            for k in range(buf.shape[0]):
+                buf[k, 0] = jnp.zeros(buf.shape[2:], BF)
+
+    @pl.when(gy == NY - 1)
+    def _():
+        for buf in (fh, ch, gh):
+            for k in range(buf.shape[0]):
+                buf[k, buf.shape[1] - 1] = jnp.zeros(buf.shape[2:], BF)
+
+    loads[3].wait()
+    loads[4].wait()
     upf[...] = up_ref[...].astype(F32)
 
     @pl.loop(0, 64)
@@ -200,9 +250,24 @@
                 axis=1,
             )
 
-    halo_arrived(*f_halo)
     first64, last64 = lane_masks(64)
     first, last = lane_masks(32)
+
+    def spread_cotangent(zi, yi):
+        row = ch[zi, yi]
+        even, odd = row[:, 0:128], row[:, 128:256]
+        at = (zi * 6 + yi) * 96
+        cx[at : at + 32, 0:128] = odd
+        cx[at : at + 32, 128:256] = after_lane(even.astype(F32), last).astype(BF)
+        cx[at + 32 : at + 64, :] = row
+        cx[at + 64 : at + 96, 0:128] = before_lane(odd.astype(F32), first).astype(BF)
+        cx[at + 64 : at + 96, 128:256] = even
+
+    for zi in range(1, 5):
+        for yi in range(1, 5):
+            spread_cotangent(zi, yi)
+
+    halo_arrived(*f_halo)
     for k in range(16):
         row = fh[k // 4, k % 4]
         wide = row.astype(F32)
@@ -257,18 +322,10 @@
             hx[zi * 576 + 480 : zi * 576 + 576] = jnp.zeros((96, 256), BF)
 
     halo_arrived(*c_halo)
-
-    @pl.loop(0, 6)
-    def _(zi):
+    for zi in range(6):
         for yi in range(6):
-            row = ch[zi, yi]
-            even_b, odd_b = row[:, 0:128], row[:, 128:256]
-            at = pl.multiple_of((zi * 6 + yi) * 96, 32)
-            cx[pl.ds(at, 32), 0:128] = odd_b
-            cx[pl.ds(at, 32), 128:256] = after_lane(even_b.astype(F32), last).astype(BF)
-            cx[pl.ds(at + 32, 32), :] = row
-            cx[pl.ds(at + 64, 32), 0:128] = before_lane(odd_b.astype(F32), first).astype(BF)
-            cx[pl.ds(at + 64, 32), 128:256] = even_b
+            if zi in (0, 5) or yi in (0, 5):
+                spread_cotangent(zi, yi)
 
     @pl.loop(0, 4)
     def _(zo):
@@ -305,10 +362,11 @@
                         )
                     )
             grad = mm_nt(jnp.concatenate(lhs, axis=1), jnp.concatenate(rhs, axis=1)).astype(BF)
-            at = (sz * 2 + sy) * 256
+            at = sz * HALF + sy * 256
             part[at : at + 128] = grad[:, 0:128]
             part[at + 128 : at + 256] = grad[:, 128:256]
-    part[1024:1536] = jnp.zeros((512, 128), BF)
+    for half in range(2):
+        part[half * HALF + 512 : (half + 1) * HALF] = jnp.zeros((HALF - 512, 128), BF)
     for dz in range(3):
         total = jnp.zeros((128, 576), F32)
         for zo in range(4):
@@ -319,8 +377,10 @@
             grad = total[0:32, dy * 96 : dy * 96 + 96]
             for yo in range(1, 4):
                 grad = grad + total[yo * 32 : yo * 32 + 32, (yo + dy) * 96 : (yo + dy) * 96 + 96]
-            at = 1024 + (dz * 3 + dy) * 32
-            part[at : at + 32, 0:96] = grad.astype(BF)
+            for half in range(2):
+                if 0 <= dz * 3 + dy - 4 * half < 5:
+                    at = half * HALF + 512 + (dz * 3 + dy - 4 * half) * 32
+                    part[at : at + 32, 0:96] = grad.astype(BF)
 
     def remote(src, dst, send, recv, device):
         return pltpu.make_async_remote_copy(
@@ -333,48 +393,65 @@
     copy0 = remote(part.at[pl.ds(other, HALF)], got0, s0_send, s0_recv, partner)
     copy0.start()
 
+    copy0.wait()
+    pair[...] = (part[pl.ds(mine, HALF), :].astype(F32) + got0[...].astype(F32)).astype(BF)
+
+    for index, step in enumerate(XY_STEPS):
+        q, device = xy_peer(step)
+        remote(
+            pair.at[pl.ds(pl.multiple_of(q * PIECE, 16), PIECE)], got1.at[index],
+            s1_send, s1_recv, device,
+        ).start()
+
     @pl.loop(0, 4)
     def _(zo):
         done = mm(t_fwd[...], hx[pl.ds(pl.multiple_of(zo * 576, 32), 1728), :])
         dec[pl.ds(pl.multiple_of(zo * 128, 16), 128), :] = done.astype(BF)
 
-    copy0.wait()
-    pair[...] = (part[pl.ds(mine, HALF), :].astype(F32) + got0[...].astype(F32)).astype(BF)
-
-    def copy1(step):
-        q, device = xy_peer(step)
-        return remote(
-            pair.at[pl.ds(pl.multiple_of(q * PIECE, 16), PIECE)], got1.at[xy],
-            s1_send.at[step], s1_recv.at[step], device,
+    joined = mm_nt(dec[...], split).astype(BF)
+    blocks = []
+    for k in range(32):
+        at = ((k // 8) * 4 + k % 4) * 32
+        half = (k // 4) % 2 * 128
+        blocks.append(
+            jnp.concatenate(
+                [joined[at : at + 16, half : half + 128], joined[at + 16 : at + 32, half : half + 128]],
+                axis=1,
+            )
         )
-
-    @pl.loop(1, 16)
-    def _(step):
-        copy1(step).start()
-
-    got1[xy] = pair[pl.ds(pl.multiple_of(xy * PIECE, 16), PIECE), :]
-    joined = mm_nt(dec[...], split).astype(BF)
-    order = one_hot(512, 512, lambda r: (r & 15) * 32 + (r >> 4))
-    dec_ref[...] = mm(order, joined).astype(BF)
-
-    @pl.loop(1, 16)
-    def _(step):
-        copy1(step).wait()
-
-    total = got1[0].astype(F32)
-    for k in range(1, 16):
+    ordered = mm(
+        one_hot(512, 512, lambda r: (r & 31) * 16 + (r >> 5)), jnp.concatenate(blocks, axis=0)
+    ).astype(BF)
+    dec_ref[0:512] = ordered[:, 0:128]
+    dec_ref[512:1024] = ordered[:, 128:256]
+
+    remote(got1, got1, s1_send, s1_recv, partner).wait_recv()
+    total = pair[pl.ds(pl.multiple_of(xy * PIECE, 16), PIECE), :].astype(F32)
+    for k in range(15):
         total = total + got1[k].astype(F32)
     got2[chip_z] = total.astype(BF)
 
-    def copy2(step):
-        _, device = z_peer(step)
-        return remote(
-            got2.at[chip_z], got2.at[chip_z], s2_send.at[step], s2_recv.at[step], device
-        )
-
-    @pl.loop(1, 8)
-    def _(step):
-        copy2(step).start()
+    here = got2.at[chip_z]
+    for step in Z_STEPS:
+        remote(here, here, s2_send, s2_recv, z_peer(step)).start()
+
+    seven = got2.at[0:7]
+    remote(seven, seven, s2_send, s2_recv, partner).wait_recv()
+
+    total = got2[0].astype(F32)
+    for k in range(1, 8):
+        total = total + got2[k].astype(F32)
+    spot = pl.multiple_of(mine + xy * PIECE, 16)
+    full[pl.ds(spot, PIECE), :] = total.astype(BF)
+
+    def pass_on(q):
+        here = full.at[pl.ds(pl.multiple_of(mine + q * PIECE, 16), PIECE)]
+        remote(here, here, s4_send, s4_recv, partner).start()
+
+    here = full.at[pl.ds(spot, PIECE)]
+    for index, step in enumerate(XY_STEPS):
+        remote(here, here, s3_send, s3_recv.at[index], xy_peer(step)[1]).start()
+    pass_on(xy)
 
     halo_arrived(*g_halo)
     for zi in range(6):
@@ -401,69 +478,74 @@
     order = one_hot(256, 256, lambda r: (r & 3) * 64 + (r >> 2))
     fgrad_ref[...] = mm(order, jnp.concatenate(flat, axis=0)).astype(BF)
 
-    @pl.loop(1, 8)
-    def _(step):
-        copy2(step).wait()
-
-    total = got2[0].astype(F32)
-    for k in range(1, 8):
-        total = total + got2[k].astype(F32)
-    spot = pl.multiple_of(mine + xy * PIECE, 16)
-    full[pl.ds(spot, PIECE), :] = total.astype(BF)
-
-    def copy3(step):
-        _, device = xy_peer(step)
-        here = full.at[pl.ds(spot, PIECE)]
-        return remote(here, here, s3_send.at[step], s3_recv.at[step], device)
-
-    @pl.loop(1, 16)
-    def _(step):
-        copy3(step).start()
-
-    @pl.loop(1, 16)
-    def _(step):
-        copy3(step).wait()
-
-    here = full.at[pl.ds(mine, HALF)]
-    copy4 = remote(here, here, s4_send, s4_recv, partner)
-    copy4.start()
+    for index in reversed(range(15)):
+        dx, dy = XY_STEPS[index]
+        remote(here, here, s3_send, s3_recv.at[index], partner).wait_recv()
+        pass_on(xy_peer((-dx, -dy))[0])
+
     halo_sent(*f_halo)
     halo_sent(*c_halo)
     halo_sent(*g_halo)
-    copy4.wait()
-
-    scale = 1.0 / math.sqrt(131072)
-    for sz in range(2):
-        for vz in range(2):
-            for sy in range(2):
-                at = ((sz * 2 + sy) * 2 + vz) * 128
-                for kx in range(4):
-                    rows = full[at + kx * 32 : at + kx * 32 + 32, :].astype(F32) * scale
-                    for vy in range(2):
-                        k = (2 * vz + sz) * 16 + (2 * vy + sy) * 4 + kx
-                        ugrad_ref[pl.ds(k, 32, stride=64), :] = rows[:, vy * 64 : vy * 64 + 64]
-    scale = 1.0 / math.sqrt(1048576)
-    for k in range(9):
-        rows = full[1024 + k * 32 : 1024 + k * 32 + 32, :].astype(F32) * scale
-        for dx in range(3):
-            at = (k * 3 + dx) * 32
-            cgrad_ref[at : at + 32, :] = rows[:, dx * 32 : dx * 32 + 32]
+    remote(got1, got1, s1_send, s1_recv, partner).wait_send()
+    remote(seven, seven, s2_send, s2_recv, partner).wait_send()
+    remote(got1, got1, s3_send, s1_recv, partner).wait_send()
+    def convert(half):
+        start = pl.multiple_of(half * HALF, 16)
+        scale = 1.0 / math.sqrt(131072)
+        for unit in range(16):
+            sy, vz, kx = unit // 8, unit // 4 % 2, unit % 4
+            rows = full[pl.ds(start + unit * 32, 32), :].astype(F32) * scale
+            for vy in range(2):
+                k = half * 16 + vz * 32 + (2 * vy + sy) * 4 + kx
+                ugrad_ref[pl.ds(k, 32, stride=64), :] = rows[:, vy * 64 : vy * 64 + 64]
+        scale = 1.0 / math.sqrt(1048576)
+        for unit in range(5):
+            rows = full[pl.ds(start + 512 + unit * 32, 32), :].astype(F32) * scale
+            for dx in range(3):
+                at = pl.multiple_of(half * 384 + (unit * 3 + dx) * 32, 8)
+                cgrad_ref[pl.ds(at, 32), :] = rows[:, dx * 32 : dx * 32 + 32]
+
+    convert(core)
+    here = full.at[pl.ds(mine, HALF)]
+    remote(here, here, s4_send, s4_recv, partner).wait()
+
+    convert(1 - core)
+
+
+def write_out(*refs):
+    sources, targets, sem = refs[0:4], refs[4:8], refs[8]
+    copies = [pltpu.make_async_copy(sources[k], targets[k], sem.at[k]) for k in range(4)]
+    for copy in copies:
+        copy.start()
+    for copy in copies:
+        copy.wait()
+
+
+def in_hbm(x):
+    return pltpu.with_memory_space_constraint(x, pltpu.HBM)
 
 
 def shards(features, up_weight, conv_weight, out_grad, labels):
     dma = pltpu.SemaphoreType.DMA
     vmem = pltpu.VMEM
-    decoded, features_grad, up_grad, conv_grad = pl.pallas_call(
+    shapes = (
+        jax.ShapeDtypeStruct((1024, 128), BF),
+        jax.ShapeDtypeStruct((256, 128), BF),
+        jax.ShapeDtypeStruct((2048, 64), F32),
+        jax.ShapeDtypeStruct((864, 32), F32),
+    )
+    results = pl.pallas_call(
         kernel,
-        out_shape=(
-            jax.ShapeDtypeStruct((512, 256), BF),
-            jax.ShapeDtypeStruct((256, 128), BF),
-            jax.ShapeDtypeStruct((2048, 64), F32),
-            jax.ShapeDtypeStruct((864, 32), F32),
-        ),
-        in_specs=[pl.BlockSpec(memory_space=vmem)] * 5,
+        out_shape=tuple(vmem(shape.shape, shape.dtype) for shape in shapes),
+        in_specs=[pl.BlockSpec(memory_space=pl.ANY)] * 5,
         out_specs=[pl.BlockSpec(memory_space=vmem)] * 4,
         scratch_shapes=[
+            vmem((256, 128), BF),
+            vmem((2048, 64), BF),
+            vmem((864, 32), BF),
+            vmem((1024, 128), BF),
+            vmem((32, 128), jnp.int32),
+            dma((5,)),
             vmem((4, 4, 64, 128), BF),
             vmem((6, 6, 32, 256), BF),
             vmem((6, 6, 32, 256), BF),
@@ -481,25 +563,34 @@
             vmem((2 * HALF, 128), BF),
             vmem((HALF, 128), BF),
             vmem((HALF, 128), BF),
-            vmem((16, PIECE, 128), BF),
+            vmem((15, PIECE, 128), BF),
             vmem((8, PIECE, 128), BF),
             vmem((2 * HALF, 128), BF),
             dma((8,)), dma((8,)), dma((8,)), dma((8,)), dma((8,)), dma((8,)),
-            dma, dma, dma((16,)), dma((16,)), dma((8,)), dma((8,)), dma((16,)), dma((16,)), dma, dma,
+            dma, dma, dma, dma, dma, dma, dma, dma((16,)), dma, dma,
         ],
         compiler_params=pltpu.CompilerParams(
-            collective_id=0, has_side_effects=True, vmem_limit_bytes=48 * 1024 * 1024
+            collective_id=0, has_side_effects=True, vmem_limit_bytes=40 * 1024 * 1024
         ),
         name="decoder_step",
     )(
-        features.reshape(256, 128),
-        jnp.transpose(up_weight, (1, 2, 3, 4, 0)).reshape(2048, 64),
-        jnp.transpose(conv_weight, (2, 3, 4, 0, 1)).reshape(864, 32),
-        out_grad.reshape(512, 256),
-        labels.reshape(16, 256),
+        in_hbm(features.reshape(256, 128)),
+        in_hbm(jnp.transpose(up_weight, (1, 2, 3, 4, 0)).reshape(2048, 64)),
+        in_hbm(jnp.transpose(conv_weight, (2, 3, 4, 0, 1)).reshape(864, 32)),
+        in_hbm(jnp.transpose(out_grad.reshape(32, 4, 4, 2, 128), (0, 1, 3, 2, 4)).reshape(1024, 128)),
+        in_hbm(jnp.transpose(labels.reshape(4, 4, 2, 128), (0, 2, 1, 3)).reshape(32, 128)),
     )
+    decoded, features_grad, up_grad, conv_grad = pl.pallas_call(
+        write_out,
+        out_shape=shapes,
+        in_specs=[pl.BlockSpec(memory_space=pl.ANY)] * 4,
+        out_specs=[pl.BlockSpec(memory_space=pl.ANY)] * 4,
+        scratch_shapes=[dma((4,))],
+        compiler_params=pltpu.CompilerParams(vmem_limit_bytes=40 * 1024 * 1024),
+        name="write_out",
+    )(*results)
     return (
-        decoded.reshape(32, 4, 4, 256),
+        jnp.transpose(decoded.reshape(32, 4, 2, 4, 128), (0, 1, 3, 2, 4)).reshape(32, 4, 4, 256),
         features_grad.reshape(64, 2, 2, 128),
         jnp.transpose(up_grad.reshape(32, 4, 4, 4, 64), (4, 0, 1, 2, 3)),
         jnp.transpose(conv_grad.reshape(3, 3, 3, 32, 32), (3, 4, 0, 1, 2)),

time: 56.5 us -> 47.5 us (0.84)
  local copies, waits for them, and re-layouts: 6.7 us -> 0 us
  Pallas kernels: 48.9 us -> 46.7 us
    unnamed x9 -> x0, local copies, waits for them, and re-layouts: 4.13 us -> none
    reshape x3 -> x0, local copies, waits for them, and re-layouts: 2.57 us -> none  [the longest x1 1.01 us: shards(): out_grad.reshape(512, 256)]
    pallas_call x1 -> x2, Pallas kernels: 48.9 us -> 46.7 us  [the longest x1 45.5 us: shards(): pl.pallas_call(kernel, out_shape=tuple((vmem(shape.shape, shape.dtype) fo...]
where the time goes in v2:
time: 47.5 us; the launch traced here: 47.4 us
  Pallas kernels  46.7 us (98%)
  between operations  0.64 us (1%)
    pallas_call x1, Pallas kernels, shards(): pl.pallas_call(kernel, out_shape=tuple((vmem(shape.shape, shape.dtype) fo...  45.5 us
    pallas_call x1, Pallas kernels, shards(): pl.pallas_call(write_out, out_shape=shapes, in_specs=[pl.BlockSpec(memory...  1.25 us

profile of v2, /device:TPU:1, one launch (start us, length us, event | category | flops | bytes accessed | tf_op | source)
XLA Modules:
  0.0 47.4 jit_solution(11180577058994902615)
XLA Ops:
  0.6 45.5 %decoder_step.1 = (bf16[1024,128]{1,0:T(8,128)(2,1)S(1)}, bf16[256,128]{1,0:T(8,128)(2,1)S(1)}, f32[2048,64]{1,0:T(8,128)S(1)}, f32[864,32]{1,0:T(8,128)S(1)}) custom-call(bf16[256,128]{1,0:T(8,128)(2,1)} %bitcast.32, bf16[2048,64]{1,0:T(8,128)(2,1)} %bitcast.29, bf16[864,32]{1,0:T(8,128)(2,1)} %bitcast.31, bf16[1024,128]{1,0:T(8,128)(2,1)} %bitcast.30, ...), custom_call_target="tpu_custom_call" | custom-call | tf_op jit(solution)/shard_map/decoder_step/pallas_call | solution.py:537
  46.1 1.3 %write_out.1 = (bf16[1024,128]{1,0:T(8,128)(2,1)}, bf16[256,128]{1,0:T(8,128)(2,1)}, f32[2048,64]{1,0:T(8,128)}, f32[864,32]{1,0:T(8,128)}) custom-call(bf16[1024,128]{1,0:T(8,128)(2,1)S(1)} %get-tuple-element.12.refs_0_, bf16[256,128]{1,0:T(8,128)(2,1)S(1)} %get-tuple-element.13.refs_1_, f32[2048,64]{1,0:T(8,128)S(1)} %get-tuple-element.14.refs_2_, ...), custom_call_target="tpu_custom_call" | custom-call | tf_op jit(solution)/shard_map/write_out/pallas_call | solution.py:583

commit v3 on v2

--- a/solution.py
+++ b/solution.py
@@ -161,11 +161,25 @@
             device_id_type=MESH,
         )
 
-    def halo_start(*what):
-        for index, (dz, dy) in enumerate(DIRECTIONS):
-            @pl.when(exists(dz, dy))
-            def _():
-                halo_copy(what[0], what[1], index, what[2], what[3]).start()
+    def halo_start(side, *halos):
+        for what in halos:
+            for index, (dz, dy) in sorted(enumerate(DIRECTIONS), key=lambda item: abs(item[1][0])):
+                if dy == side:
+                    @pl.when(exists(dz, dy))
+                    def _():
+                        halo_copy(what[0], what[1], index, what[2], what[3]).start()
+
+    def halo_start_all(*halos):
+        @pl.when(gy % 16 == 0)
+        def _():
+            halo_start(-1, *halos)
+
+        halo_start(1, *halos)
+        halo_start(0, *halos)
+
+        @pl.when(gy % 16 > 0)
+        def _():
+            halo_start(-1, *halos)
 
     def halo_arrived(*what):
         for index, (dz, dy) in enumerate(DIRECTIONS):
@@ -182,8 +196,7 @@
     f_halo = (fh, 2, f_send, f_recv)
     c_halo = (ch, 4, c_send, c_recv)
     g_halo = (gh, 4, g_send, g_recv)
-    halo_start(*f_halo)
-    halo_start(*c_halo)
+    halo_start_all(f_halo, c_halo)
 
     @pl.when(gz == 0)
     def _():
@@ -275,8 +288,7 @@
         fx[k, 64:128] = row
         fx[k, 128:192] = after_lane(wide, last64).astype(BF)
 
-    @pl.loop(0, 3)
-    def _(jz):
+    for jz in range(3):
         columns = []
         for jy in range(3):
             columns.append(
@@ -292,7 +304,7 @@
                     even = lifted[at : at + 32, jy * 128 : jy * 128 + 128]
                     odd = lifted[at + 32 : at + 64, jy * 128 : jy * 128 + 128]
                     zo, yo = jz * 2 + sz, jy * 2 + sy
-                    at = pl.multiple_of((zo * 6 + yo) * 96, 32)
+                    at = (zo * 6 + yo) * 96
                     even_b, odd_b = even.astype(BF), odd.astype(BF)
                     hx[pl.ds(at, 32), 0:128] = before_lane(odd, first).astype(BF)
                     hx[pl.ds(at, 32), 128:256] = even_b
@@ -321,22 +333,52 @@
         for zi in range(6):
             hx[zi * 576 + 480 : zi * 576 + 576] = jnp.zeros((96, 256), BF)
 
+    def remote(src, dst, send, recv, device):
+        return pltpu.make_async_remote_copy(
+            src_ref=src, dst_ref=dst, send_sem=send, recv_sem=recv,
+            device_id=device, device_id_type=MESH,
+        )
+
+    mine = pl.multiple_of(core * HALF, 16)
+    other = pl.multiple_of((1 - core) * HALF, 16)
+    for half in range(2):
+        part[half * HALF + 512 : (half + 1) * HALF] = jnp.zeros((HALF - 512, 128), BF)
+    for dz in range(3):
+        total = mm_nt(
+            jnp.concatenate([hx[(zo + dz) * 576 : (zo + dz + 1) * 576, :] for zo in range(4)], axis=1),
+            jnp.concatenate([ch[1 + zo, 1:5].reshape(128, 256) for zo in range(4)], axis=1),
+        )
+        for dy in range(3):
+            grad = total[dy * 96 : dy * 96 + 96, 0:32]
+            for yo in range(1, 4):
+                grad = grad + total[(yo + dy) * 96 : (yo + dy) * 96 + 96, yo * 32 : yo * 32 + 32]
+            grad = grad.T
+            for half in range(2):
+                if 0 <= dz * 3 + dy - 4 * half < 5:
+                    at = half * HALF + 512 + (dz * 3 + dy - 4 * half) * 32
+                    part[at : at + 32, 0:96] = grad.astype(BF)
+
+    copy_conv = remote(
+        part.at[pl.ds(pl.multiple_of(other + 512, 16), 256)], got0.at[512:768],
+        s0_send.at[0], s0_recv.at[0], partner,
+    )
+    copy_conv.start()
+
     halo_arrived(*c_halo)
     for zi in range(6):
         for yi in range(6):
             if zi in (0, 5) or yi in (0, 5):
                 spread_cotangent(zi, yi)
 
-    @pl.loop(0, 4)
-    def _(zo):
-        before = mm(t_bwd[...], cx[pl.ds(pl.multiple_of(zo * 576, 32), 1728), :])
+    for zo in range(4):
+        before = mm(t_bwd[...], cx[pl.ds(zo * 576, 1728), :])
         for yo in range(4):
             grad = jnp.where(
                 he[1 + zo, 1 + yo].astype(F32) > 0.0, before[yo * 32 : yo * 32 + 32], 0.0
             )
             gh[1 + zo, 1 + yo] = grad.astype(BF)
 
-    halo_start(*g_halo)
+    halo_start_all(g_halo)
 
     def spread_grad(row, slot):
         even, odd = row[:, 0:128], row[:, 128:256]
@@ -365,35 +407,13 @@
             at = sz * HALF + sy * 256
             part[at : at + 128] = grad[:, 0:128]
             part[at + 128 : at + 256] = grad[:, 128:256]
-    for half in range(2):
-        part[half * HALF + 512 : (half + 1) * HALF] = jnp.zeros((HALF - 512, 128), BF)
-    for dz in range(3):
-        total = jnp.zeros((128, 576), F32)
-        for zo in range(4):
-            total = total + mm_nt(
-                ch[1 + zo, 1:5].reshape(128, 256), hx[(zo + dz) * 576 : (zo + dz + 1) * 576, :]
-            )
-        for dy in range(3):
-            grad = total[0:32, dy * 96 : dy * 96 + 96]
-            for yo in range(1, 4):
-                grad = grad + total[yo * 32 : yo * 32 + 32, (yo + dy) * 96 : (yo + dy) * 96 + 96]
-            for half in range(2):
-                if 0 <= dz * 3 + dy - 4 * half < 5:
-                    at = half * HALF + 512 + (dz * 3 + dy - 4 * half) * 32
-                    part[at : at + 32, 0:96] = grad.astype(BF)
-
-    def remote(src, dst, send, recv, device):
-        return pltpu.make_async_remote_copy(
-            src_ref=src, dst_ref=dst, send_sem=send, recv_sem=recv,
-            device_id=device, device_id_type=MESH,
-        )
-
-    mine = pl.multiple_of(core * HALF, 16)
-    other = pl.multiple_of((1 - core) * HALF, 16)
-    copy0 = remote(part.at[pl.ds(other, HALF)], got0, s0_send, s0_recv, partner)
-    copy0.start()
-
-    copy0.wait()
+    copy_up = remote(
+        part.at[pl.ds(other, 512)], got0.at[0:512], s0_send.at[1], s0_recv.at[1], partner
+    )
+    copy_up.start()
+
+    copy_conv.wait()
+    copy_up.wait()
     pair[...] = (part[pl.ds(mine, HALF), :].astype(F32) + got0[...].astype(F32)).astype(BF)
 
     for index, step in enumerate(XY_STEPS):
@@ -403,10 +423,9 @@
             s1_send, s1_recv, device,
         ).start()
 
-    @pl.loop(0, 4)
-    def _(zo):
-        done = mm(t_fwd[...], hx[pl.ds(pl.multiple_of(zo * 576, 32), 1728), :])
-        dec[pl.ds(pl.multiple_of(zo * 128, 16), 128), :] = done.astype(BF)
+    for zo in range(4):
+        done = mm(t_fwd[...], hx[pl.ds(zo * 576, 1728), :])
+        dec[pl.ds(zo * 128, 128), :] = done.astype(BF)
 
     joined = mm_nt(dec[...], split).astype(BF)
     blocks = []
@@ -567,7 +586,7 @@
             vmem((8, PIECE, 128), BF),
             vmem((2 * HALF, 128), BF),
             dma((8,)), dma((8,)), dma((8,)), dma((8,)), dma((8,)), dma((8,)),
-            dma, dma, dma, dma, dma, dma, dma, dma((16,)), dma, dma,
+            dma((2,)), dma((2,)), dma, dma, dma, dma, dma, dma((16,)), dma, dma,
         ],
         compiler_params=pltpu.CompilerParams(
             collective_id=0, has_side_effects=True, vmem_limit_bytes=40 * 1024 * 1024

time: 47.5 us -> 45.9 us (0.966)
  Pallas kernels: 46.7 us -> 45.1 us
    pallas_call x1, Pallas kernels: 45.5 us -> 43.9 us  [shards(): pl.pallas_call(kernel, out_shape=tuple((vmem(shape.shape, shape.dtype) fo...]
where the time goes in v3:
time: 45.9 us; the launch traced here: 45.8 us
  Pallas kernels  45.1 us (98%)
  between operations  0.64 us (1%)
    pallas_call x1, Pallas kernels, shards(): pl.pallas_call(kernel, out_shape=tuple((vmem(shape.shape, shape.dtype) fo...  43.9 us
    pallas_call x1, Pallas kernels, shards(): pl.pallas_call(write_out, out_shape=shapes, in_specs=[pl.BlockSpec(memory...  1.25 us

profile of v3, /device:TPU:1, one launch (start us, length us, event | category | flops | bytes accessed | tf_op | source)
XLA Modules:
  0.0 45.8 jit_solution(17920631951813312190)
XLA Ops:
  0.6 43.9 %decoder_step.1 = (bf16[1024,128]{1,0:T(8,128)(2,1)S(1)}, bf16[256,128]{1,0:T(8,128)(2,1)S(1)}, f32[2048,64]{1,0:T(8,128)S(1)}, f32[864,32]{1,0:T(8,128)S(1)}) custom-call(bf16[256,128]{1,0:T(8,128)(2,1)} %bitcast.32, bf16[2048,64]{1,0:T(8,128)(2,1)} %bitcast.29, bf16[864,32]{1,0:T(8,128)(2,1)} %bitcast.31, bf16[1024,128]{1,0:T(8,128)(2,1)} %bitcast.30, ...), custom_call_target="tpu_custom_call" | custom-call | tf_op jit(solution)/shard_map/decoder_step/pallas_call | solution.py:556
  44.5 1.3 %write_out.1 = (bf16[1024,128]{1,0:T(8,128)(2,1)}, bf16[256,128]{1,0:T(8,128)(2,1)}, f32[2048,64]{1,0:T(8,128)}, f32[864,32]{1,0:T(8,128)}) custom-call(bf16[1024,128]{1,0:T(8,128)(2,1)S(1)} %get-tuple-element.12.refs_0_, bf16[256,128]{1,0:T(8,128)(2,1)S(1)} %get-tuple-element.13.refs_1_, f32[2048,64]{1,0:T(8,128)S(1)} %get-tuple-element.14.refs_2_, ...), custom_call_target="tpu_custom_call" | custom-call | tf_op jit(solution)/shard_map/write_out/pallas_call | solution.py:602

commit v4 on v3

--- a/solution.py
+++ b/solution.py
@@ -12,7 +12,7 @@
 MESH = pl.DeviceIdType.MESH
 
 NZ, NY = 8, 32
-DIRECTIONS = [(dz, dy) for dz in (-1, 0, 1) for dy in (-1, 0, 1) if (dz, dy) != (0, 0)]
+DIRECTIONS = [(0, 1), (0, -1), (1, 1), (-1, 1), (1, -1), (-1, -1), (1, 0), (-1, 0)]
 XY_STEPS = sorted(
     [(dx, dy) for dx in range(4) for dy in range(4) if (dx, dy) != (0, 0)],
     key=lambda step: -(min(step[0], 4 - step[0]) + min(step[1], 4 - step[1])),
@@ -118,7 +118,11 @@
     pl.semaphore_signal(barrier, 1, device_id=partner, device_id_type=MESH)
 
     for step in XY_STEPS:
-        pl.semaphore_signal(barrier, 1, device_id=xy_peer(step)[1], device_id_type=MESH)
+        q, device = xy_peer(step)
+        pl.semaphore_signal(barrier, 1, device_id=device, device_id_type=MESH)
+        pl.semaphore_signal(
+            barrier, 1, device_id=(partner[0], z_hi * 16 + q), device_id_type=MESH
+        )
     for step in Z_STEPS:
         pl.semaphore_signal(barrier, 1, device_id=z_peer(step), device_id_type=MESH)
 
@@ -148,7 +152,7 @@
 
     beside = 1 * (gz > 0) + 1 + 1 * (gz < NZ - 1)
     beside = beside * (1 * (gy > 0) + 1 + 1 * (gy < NY - 1)) - 1
-    pl.semaphore_wait(barrier, beside + 1 + 15 + 7)
+    pl.semaphore_wait(barrier, beside + 1 + 30 + 7)
 
     def halo_copy(buf, extent, index, send, recv):
         dz, dy = DIRECTIONS[index]
@@ -391,10 +395,11 @@
         for yi in range(1, 5):
             spread_grad(gh[zi, yi], zi * 6 + yi)
 
-    for sz in range(2):
+    def up_terms(sz):
         for sy in range(2):
             lhs, rhs = [], []
-            for jz in (0, 1) if sz else (1, 2):
+            for turn in range(2):
+                jz = turn + 1 - sz
                 for jy in (0, 1) if sy else (1, 2):
                     lhs.append(hgx[(2 * jz + sz) * 6 + 2 * jy + sy])
                     rhs.append(
@@ -404,14 +409,16 @@
                         )
                     )
             grad = mm_nt(jnp.concatenate(lhs, axis=1), jnp.concatenate(rhs, axis=1)).astype(BF)
-            at = sz * HALF + sy * 256
-            part[at : at + 128] = grad[:, 0:128]
-            part[at + 128 : at + 256] = grad[:, 128:256]
+            at = pl.multiple_of(sz * HALF + sy * 256, 16)
+            part[pl.ds(at, 128), :] = grad[:, 0:128]
+            part[pl.ds(at + 128, 128), :] = grad[:, 128:256]
+
+    up_terms(1 - core)
     copy_up = remote(
         part.at[pl.ds(other, 512)], got0.at[0:512], s0_send.at[1], s0_recv.at[1], partner
     )
     copy_up.start()
-
+    up_terms(core)
     copy_conv.wait()
     copy_up.wait()
     pair[...] = (part[pl.ds(mine, HALF), :].astype(F32) + got0[...].astype(F32)).astype(BF)
@@ -463,14 +470,12 @@
     spot = pl.multiple_of(mine + xy * PIECE, 16)
     full[pl.ds(spot, PIECE), :] = total.astype(BF)
 
-    def pass_on(q):
-        here = full.at[pl.ds(pl.multiple_of(mine + q * PIECE, 16), PIECE)]
-        remote(here, here, s4_send, s4_recv, partner).start()
-
     here = full.at[pl.ds(spot, PIECE)]
     for index, step in enumerate(XY_STEPS):
-        remote(here, here, s3_send, s3_recv.at[index], xy_peer(step)[1]).start()
-    pass_on(xy)
+        q, device = xy_peer(step)
+        remote(here, here, s3_send, s3_recv.at[index], device).start()
+        remote(here, here, s4_send, s4_recv, (partner[0], z_hi * 16 + q)).start()
+    remote(here, here, s4_send, s4_recv, partner).start()
 
     halo_arrived(*g_halo)
     for zi in range(6):
@@ -498,9 +503,7 @@
     fgrad_ref[...] = mm(order, jnp.concatenate(flat, axis=0)).astype(BF)
 
     for index in reversed(range(15)):
-        dx, dy = XY_STEPS[index]
         remote(here, here, s3_send, s3_recv.at[index], partner).wait_recv()
-        pass_on(xy_peer((-dx, -dy))[0])
 
     halo_sent(*f_halo)
     halo_sent(*c_halo)

time: 45.9 us -> 45.2 us (0.985)
  Pallas kernels: 45.1 us -> 44.5 us
    pallas_call x1, Pallas kernels: 43.9 us -> 43.2 us  [shards(): pl.pallas_call(kernel, out_shape=tuple((vmem(shape.shape, shape.dtype) fo...]
where the time goes in v4:
time: 45.2 us; the launch traced here: 45.1 us
  Pallas kernels  44.5 us (98%)
  between operations  0.64 us (1%)
    pallas_call x1, Pallas kernels, shards(): pl.pallas_call(kernel, out_shape=tuple((vmem(shape.shape, shape.dtype) fo...  43.2 us
    pallas_call x1, Pallas kernels, shards(): pl.pallas_call(write_out, out_shape=shapes, in_specs=[pl.BlockSpec(memory...  1.25 us

profile of v4, /device:TPU:1, one launch (start us, length us, event | category | flops | bytes accessed | tf_op | source)
XLA Modules:
  0.0 45.1 jit_solution(15967595934146673163)
XLA Ops:
  0.6 43.2 %decoder_step.1 = (bf16[1024,128]{1,0:T(8,128)(2,1)S(1)}, bf16[256,128]{1,0:T(8,128)(2,1)S(1)}, f32[2048,64]{1,0:T(8,128)S(1)}, f32[864,32]{1,0:T(8,128)S(1)}) custom-call(bf16[256,128]{1,0:T(8,128)(2,1)} %bitcast.32, bf16[2048,64]{1,0:T(8,128)(2,1)} %bitcast.29, bf16[864,32]{1,0:T(8,128)(2,1)} %bitcast.31, bf16[1024,128]{1,0:T(8,128)(2,1)} %bitcast.30, ...), custom_call_target="tpu_custom_call" | custom-call | tf_op jit(solution)/shard_map/decoder_step/pallas_call | solution.py:559
  43.9 1.3 %write_out.1 = (bf16[1024,128]{1,0:T(8,128)(2,1)}, bf16[256,128]{1,0:T(8,128)(2,1)}, f32[2048,64]{1,0:T(8,128)}, f32[864,32]{1,0:T(8,128)}) custom-call(bf16[1024,128]{1,0:T(8,128)(2,1)S(1)} %get-tuple-element.12.refs_0_, bf16[256,128]{1,0:T(8,128)(2,1)S(1)} %get-tuple-element.13.refs_1_, f32[2048,64]{1,0:T(8,128)S(1)} %get-tuple-element.14.refs_2_, ...), custom_call_target="tpu_custom_call" | custom-call | tf_op jit(solution)/shard_map/write_out/pallas_call | solution.py:605
